TPU v7x, 256 devices: a whole 4x4x8 slice. The times are simulated.
256 devices in a mesh: gx: 32 (over z, y), gz: 8 (over x, core).
Axes of the slice: x: 4, y: 4, z: 8, core: 2. Of those that a mesh axis runs over, the one named last changes fastest.
Arguments:
- velocity: float32 [3, 8, 8192, 2048], P(None, None, 'gx', 'gz'), may hold values from -18 to 18
Outputs:
- derivative: float32 [3, 8, 8192, 2048], P(None, None, 'gx', 'gz')
- energy: float32 [3, 8], replicated
All inputs are finite; a program needn't handle non-finite values.
Results may differ from a plain program's by a relative error of at most 0.00017.
Values sent between devices are 32-bit elements; how exact they have to be, the bound alone decides.
A program may use at most 64 MiB of HBM per device.

v0:
```python
import math

import jax
import jax.numpy as jnp
from jax import lax
from jax.sharding import PartitionSpec as P

ALPHA = 1.0 / 3.0
HALF_A = 7.0 / 9.0
QUARTER_B = 1.0 / 36.0


def padded_2(cells, sides, width):
    for axis, dim in sides:
        count = lax.axis_size(axis)
        head = lax.slice_in_dim(cells, 0, width, axis=dim)
        tail = lax.slice_in_dim(cells, cells.shape[dim] - width, cells.shape[dim], axis=dim)
        cells = jnp.concatenate(
            [
                lax.ppermute(tail, axis, [(i, (i + 1) % count) for i in range(count)]),
                cells,
                lax.ppermute(head, axis, [((i + 1) % count, i) for i in range(count)]),
            ],
            axis=dim,
        )
    return cells


def shifted(block, axis, distance):
    devices = range(lax.axis_size(axis))
    route = [((i - distance) % len(devices), i) for i in devices]
    return lax.ppermute(block, axis, route)


def local_inverse(points):
    root_term = math.sqrt(1.0 - 4.0 * ALPHA * ALPHA)
    log_larger = math.log(0.5 * (1.0 + root_term))
    log_ratio = math.log((1.0 - root_term) / (1.0 + root_term))
    log_spread = math.log(root_term)

    def log_theta(order):
        return (
            (order + 1.0) * log_larger + jnp.log1p(-jnp.exp((order + 1.0) * log_ratio)) - log_spread
        )

    row_ids = lax.broadcasted_iota(jnp.float32, (points, points), 0)
    column_ids = lax.broadcasted_iota(jnp.float32, (points, points), 1)
    lower = jnp.minimum(row_ids, column_ids)
    upper = jnp.maximum(row_ids, column_ids)
    distance = upper - lower
    magnitude = jnp.exp(
        distance * math.log(ALPHA)
        + log_theta(lower)
        + log_theta(points - 1.0 - upper)
        - log_theta(jnp.float32(points))
    )
    parity = 1.0 - 2.0 * jnp.mod(distance, 2.0)
    return parity * magnitude


def stencil(padded, count):
    return HALF_A * (padded[:, :, 3 : count + 3] - padded[:, :, 1 : count + 1]) + QUARTER_B * (
        padded[:, :, 4 : count + 4] - padded[:, :, 0:count]
    )


def edge_solve(padded, points):
    right_side = stencil(padded, points)
    inverse = local_inverse(points)
    solved = jnp.einsum("ij,cpjz->cpiz", inverse, right_side, precision=lax.Precision.HIGHEST)
    return (inverse, solved)


def shards(velocity):
    components, planes, points, spanwise = velocity.shape
    padded = padded_2(velocity, (("gx", 2),), 2)
    inverse, solved = edge_solve(padded, points)
    coupling = ALPHA * inverse[0, 0]
    denominator = 1.0 - coupling * coupling
    first_edge = solved[:, :, 0]
    last_edge = solved[:, :, points - 1]
    from_left = shifted(last_edge, "gx", 1)
    from_right = shifted(first_edge, "gx", -1)
    left_value = (from_left - coupling * first_edge) / denominator
    right_value = (from_right - coupling * last_edge) / denominator
    first_column = inverse[:, 0]
    last_column = inverse[:, points - 1]
    derivative = solved - ALPHA * (
        first_column[None, None, :, None] * left_value[:, :, None, :]
        + last_column[None, None, :, None] * right_value[:, :, None, :]
    )
    local_sums = jnp.sum(derivative * derivative, axis=(2, 3))
    totals = lax.psum(local_sums, ("gx", "gz"))
    energy = totals / float(points * lax.axis_size("gx") * spanwise * lax.axis_size("gz"))
    return (derivative, energy)


def solution(mesh):
    return jax.shard_map(
        shards,
        mesh=mesh,
        in_specs=(P(None, None, "gx", "gz"),),
        out_specs=(P(None, None, "gx", "gz"), P()),
        check_vma=False,
    )
```

profile of v0, /device:TPU:1, one launch (start us, length us, event | category | flops | bytes accessed | tf_op | source)
XLA Modules:
  0.0 117.0 jit_solution(6096472465696574208)
XLA Ops:
  0.6 1.1 fusion.61
  1.7 2.2 %collective-permute-start.1 = (f32[3,8,2,256]{3,2,1,0:T(2,128)S(1)}, f32[3,8,2,256]{3,2,1,0:T(2,128)S(1)}, u32[]{:S(2)}, u32[]{:S(2)}) collective-permute-start(f32[3,8,2,256]{3,2,1,0:T(2,128)S(1)} %get-tuple-element.7), channel_id=1, source_target_pairs={{0,8},{8,16},{16,24},{24,32},{32,40},{40,48},{48,56},{56,64},{64,7... | collective-permute-start | bytes 147464 | tf_op jit(solution)/shard_map/ppermute | solution.py:20
  3.9 0.0 slice-start
  3.9 0.0 slice-start.1
  3.9 6.8 %collective-permute-start = (f32[3,8,2,256]{3,2,1,0:T(2,128)S(1)}, f32[3,8,2,256]{3,2,1,0:T(2,128)S(1)}, u32[]{:S(2)}, u32[]{:S(2)}) collective-permute-start(f32[3,8,2,256]{3,2,1,0:T(2,128)S(1)} %get-tuple-element.6), channel_id=1, source_target_pairs={{8,0},{16,8},{24,16},{32,24},{40,32},{48,40},{56,48},{64,56},{72,6... | collective-permute-start | bytes 147464 | tf_op jit(solution)/shard_map/ppermute | solution.py:22
  10.7 3.4 %constant_dynamic-update-slice_fusion.1 = f32[3,8,258,256]{3,2,1,0:T(8,128)S(1)} fusion(f32[3,8,256,256]{3,2,1,0:T(8,128)} %param.1), kind=kLoop, calls=%fused_computation.56 | loop fusion | bytes 12582912
  14.1 0.6 fusion.33
  14.7 0.0 collective-permute-done
  14.7 0.0 collective-permute-done.1
  14.7 0.0 slice-done
  14.7 0.0 slice-done.1
  14.8 9.8 %fusion.14 = f32[3,8,256,256]{3,2,1,0:T(8,128)S(1)} fusion(f32[3,8,2,256]{3,2,1,0:T(2,128)S(1)} %collective-permute-done.1, f32[3,8,256,256]{3,2,1,0:T(8,128)S(1)} %bitcast.20, f32[3,8,258,256]{3,2,1,0:T(8,128)S(1)} %constant_dynamic-update-slice_fusion), kind=kOutput, calls=%fused_computation.17 | convolution fusion | flops 4844683264 | bytes 25214976 | tf_op jit(solution)/shard_map/ij,cpjz->cpiz/dot_general | solution.py:70
  24.7 2.4 %collective-permute-start.3 = (f32[3,8,256]{2,1,0:T(8,128)S(1)}, f32[3,8,256]{2,1,0:T(8,128)S(1)}, u32[]{:S(2)}, u32[]{:S(2)}) collective-permute-start(f32[3,8,256]{2,1,0:T(8,128)S(1)} %bitcast.21), channel_id=1, source_target_pairs={{8,0},{16,8},{24,16},{32,24},{40,32},{48,40},{56,48},{64,56},{72,6... | collective-permute-start | bytes 73736 | tf_op jit(solution)/shard_map/ppermute | solution.py:32
  27.0 0.5 slice.54
  29.5 0.3 collective-permute-start.2
  29.8 0.0 collective-permute-done.3
  29.8 6.0 %collective-permute-done.2 = f32[3,8,256]{2,1,0:T(8,128)S(1)} collective-permute-done((f32[3,8,256]{2,1,0:T(8,128)S(1)}, f32[3,8,256]{2,1,0:T(8,128)S(1)}, u32[]{:S(2)}, u32[]{:S(2)}) %collective-permute-start.2) | collective-permute-done | bytes 24608 | tf_op jit(solution)/shard_map/ppermute | solution.py:32
  35.8 4.4 %multiply_reduce_fusion = (f32[3,8]{1,0:T(4,128)S(1)}, f32[3,8,256,256]{3,2,1,0:T(8,128)}) fusion(f32[3,8,256,256]{3,2,1,0:T(8,128)S(1)} %fusion.14, f32[3,8,256]{2,1,0:T(8,128)S(1)} %subtract_divide_fusion, f32[256]{0:T(256)S(1)} %bitcast.24, f32[3,8,256]{2,1,0:T(8,128)S(1)} %subtract_divide_fusion.1, f32[256]{0:T(256)S(1)} %bitcast.23), kind=kLoop, calls=%fused_computation.13 | loop fusion | flops 11010024 | bytes 12634208 | tf_op jit(solution)/shard_map/reduce_sum | solution.py:92
  40.1 76.3 %psum.7 = f32[3,8]{1,0:T(4,128)S(1)} all-reduce(f32[3,8]{1,0:T(4,128)S(1)} %get-tuple-element.2), channel_id=1, replica_groups=mesh['gx'=32,'gz'=8] {'gx','gz'}, use_global_device_ids=true, to_apply=%region_1.2 | all-reduce | flops 24 | bytes 192 | tf_op jit(solution)/shard_map/psum | solution.py:93
  116.4 0.6 broadcast_multiply_fusion
  (8 shorter events, 0.1 us)
Async XLA Ops:
  1.7 13.0 %collective-permute-start.1 = (f32[3,8,2,256]{3,2,1,0:T(2,128)S(1)}, f32[3,8,2,256]{3,2,1,0:T(2,128)S(1)}, u32[]{:S(2)}, u32[]{:S(2)}) collective-permute-start(f32[3,8,2,256]{3,2,1,0:T(2,128)S(1)} %get-tuple-element.7), channel_id=1, source_target_pairs={{0,8},{8,16},{16,24},{24,32},{32,40},{40,48},{48,56},{56,64},{64,7... | collective-permute-start | bytes 147464 | tf_op jit(solution)/shard_map/ppermute | solution.py:20
  3.9 10.8 %slice-start = ((s8[6291456]{0:T(1024)(128)(4,1)}), s8[4194304]{0:T(1024)(128)(4,1)S(1)}, s32[]{:S(2)}) async-start(s8[6291456]{0:T(1024)(128)(4,1)} %bitcast.19), calls=%async_computation | async-start | bytes 8388608
  3.9 10.9 %slice-start.1 = ((s8[6291456]{0:T(1024)(128)(4,1)}), s8[2097152]{0:T(1024)(128)(4,1)S(1)}, s32[]{:S(2)}) async-start(s8[6291456]{0:T(1024)(128)(4,1)} %bitcast.19), calls=%async_computation.1 | async-start | bytes 4194304
  3.9 10.8 %collective-permute-start = (f32[3,8,2,256]{3,2,1,0:T(2,128)S(1)}, f32[3,8,2,256]{3,2,1,0:T(2,128)S(1)}, u32[]{:S(2)}, u32[]{:S(2)}) collective-permute-start(f32[3,8,2,256]{3,2,1,0:T(2,128)S(1)} %get-tuple-element.6), channel_id=1, source_target_pairs={{8,0},{16,8},{24,16},{32,24},{40,32},{48,40},{56,48},{64,56},{72,6... | collective-permute-start | bytes 147464 | tf_op jit(solution)/shard_map/ppermute | solution.py:22
  24.7 5.1 %collective-permute-start.3 = (f32[3,8,256]{2,1,0:T(8,128)S(1)}, f32[3,8,256]{2,1,0:T(8,128)S(1)}, u32[]{:S(2)}, u32[]{:S(2)}) collective-permute-start(f32[3,8,256]{2,1,0:T(8,128)S(1)} %bitcast.21), channel_id=1, source_target_pairs={{8,0},{16,8},{24,16},{32,24},{40,32},{48,40},{56,48},{64,56},{72,6... | collective-permute-start | bytes 73736 | tf_op jit(solution)/shard_map/ppermute | solution.py:32
  29.5 6.3 %collective-permute-start.2 = (f32[3,8,256]{2,1,0:T(8,128)S(1)}, f32[3,8,256]{2,1,0:T(8,128)S(1)}, u32[]{:S(2)}, u32[]{:S(2)}) collective-permute-start(f32[3,8,256]{2,1,0:T(8,128)S(1)} %bitcast.22), channel_id=1, source_target_pairs={{248,0},{0,8},{8,16},{16,24},{24,32},{32,40},{40,48},{48,56},{56,6... | collective-permute-start | bytes 73736 | tf_op jit(solution)/shard_map/ppermute | solution.py:32
where the time goes:
time: 117 us
  blocking collectives  76.3 us (65%)
  starting transfers between devices  11.7 us (10%)
  matrix products  9.82 us (8%)
  waiting for transfers between devices  5.96 us (5%)
  other arithmetic  5.54 us (5%)
  local copies, waits for them, and re-layouts  5.03 us (4%)
  between operations  2.7 us (2%)
    psum x1, blocking collectives, shards(): totals = lax.psum(local_sums, ('gx', 'gz'))  76.3 us
    dot_general x1, matrix products, edge_solve(): jnp.einsum('ij,cpjz->cpiz', inverse, right_side, precision=lax.Precision....  9.82 us
    ppermute x1, starting transfers between devices, padded_2(): lax.ppermute(head, axis, [((i + 1) % count, i) for i in range(count)])  6.84 us
    ppermute x2, waiting for transfers between devices, shifted(): return lax.ppermute(block, axis, route)  5.95 us
    reduce_sum x1, other arithmetic, shards(): local_sums = jnp.sum(derivative * derivative, axis=(2, 3))  4.38 us
    unnamed x7, local copies, waits for them, and re-layouts  3.39 us
    ppermute x2, starting transfers between devices, shifted(): return lax.ppermute(block, axis, route)  2.64 us
  transfers between devices with their start and end apart: 4, of which 1 were waited for; matrix products, arithmetic and copies ran while one was open for 4% of the time, Pallas kernels for 0%

commit v1 on v0

v1 whole, which is shorter than its diff:
```python
import functools
import itertools
import math

import jax
import jax.numpy as jnp
import numpy as np
from jax import lax
from jax.experimental import pallas as pl
from jax.experimental.pallas import tpu as pltpu
from jax.sharding import PartitionSpec as P

ALPHA = 1.0 / 3.0
HALF_A = 7.0 / 9.0
QUARTER_B = 1.0 / 36.0

ROOT = (math.sqrt(1.0 - 4.0 * ALPHA * ALPHA) - 1.0) / (2.0 * ALPHA)
SCALE = 1.0 / math.sqrt(1.0 - 4.0 * ALPHA * ALPHA)
TAIL = SCALE * (HALF_A + QUARTER_B * (ROOT + 1.0 / ROOT))
CENTRE = SCALE * (HALF_A + 2.0 * QUARTER_B * ROOT)
BUMP = CENTRE - TAIL
REACH = 96

SIZES = {"x": 4, "y": 4, "z": 8, "core": 2}
PHASES = (("x", "y"), ("z", "core"))
MESH = pl.DeviceIdType.MESH
LANES = 128


def hops(offset, axis):
    return 0 if axis == "core" else min(offset, SIZES[axis] - offset)


def partners(axes):
    gx, gz = lax.axis_index("gx"), lax.axis_index("gz")
    here = {"x": gz // 2, "core": gz % 2, "z": gx // 4, "y": gx % 4}
    offsets = [o for o in itertools.product(*(range(SIZES[a]) for a in axes)) if any(o)]
    offsets.sort(key=lambda o: -sum(hops(v, a) for v, a in zip(o, axes)))
    found = []
    for offset in offsets:
        there = dict(here)
        for axis, value in zip(axes, offset):
            if value:
                there[axis] = (here[axis] + value) % SIZES[axis]
        found.append((there["z"] * 4 + there["y"], there["x"] * 2 + there["core"]))
    return found


def tables(points):
    index = np.arange(points)
    distance = np.abs(index[:, None] - index[None, :])
    matrix = np.where(distance == 0, CENTRE, TAIL * ROOT ** distance.astype(np.float64))
    matrix[:, 0] = 0.0
    matrix[:, points - 1] = 0.0
    reach = np.arange(REACH)
    powers = ROOT ** reach.astype(np.float64)
    head = ROOT ** (reach + 1.0)
    head[0] = head[REACH - 1] = 0.0
    columns = np.stack([powers, powers[::-1], head, head[::-1]])
    columns = np.broadcast_to(columns[:, :, None], (4, REACH, LANES))
    return matrix.astype(np.float32), columns.astype(np.float32)


def column_sum(weights, block):
    w = jnp.concatenate([weights, weights], axis=1)
    return jnp.sum(w * block, axis=0, keepdims=True)


def kernel(
    planes, points, v_hbm, matrix_hbm, column_hbm, d_ref, e_ref,
    v, matrix, high, low, columns, out, got, rows, tots, shares, load_sem, const_sem, halo_send, halo_recv, sum_send, sum_recv,
):
    gx, gz = lax.axis_index("gx"), lax.axis_index("gz")
    ring = lax.axis_size("gx")
    right, left = ((gx + 1) % ring, gz), ((gx + ring - 1) % ring, gz)
    groups = [partners(axes) for axes in PHASES]

    barrier = pltpu.get_barrier_semaphore()
    known = [left, right] + groups[0] + groups[1]
    for device in known:
        pl.semaphore_signal(barrier, inc=1, device_id=device, device_id_type=MESH)

    constants = [
        pltpu.make_async_copy(source, target, const_sem.at[i])
        for i, (source, target) in enumerate(((column_hbm, columns), (matrix_hbm, matrix)))
    ]

    def load(p):
        return pltpu.make_async_copy(v_hbm.at[p], v.at[p], load_sem.at[p])

    constants[0].start()
    for p in range(planes):
        load(p).start()
    constants[1].start()
    constants[0].wait()

    def summarise(p, carry):
        load(p).wait()
        head, tail = v[p, :REACH, :], v[p, points - REACH :, :]
        first, second = head[0:1], head[1:2]
        last, before = tail[REACH - 1 :], tail[REACH - 2 : REACH - 1]
        head = pltpu.roll(head, REACH - 1, 0) - pltpu.roll(head, 1, 0)
        tail = pltpu.roll(tail, REACH - 1, 0) - pltpu.roll(tail, 1, 0)
        one = pl.ds(p, 1)
        out[0, 0, one, :] = first
        out[0, 1, one, :] = column_sum(columns[2], head) + ROOT * (second - first)
        out[1, 0, one, :] = last
        out[1, 1, one, :] = column_sum(columns[3], tail) + ROOT * (last - before)
        rows[0, one, :] = second
        rows[1, one, :] = before
        return carry

    lax.fori_loop(0, planes, summarise, 0)

    pl.semaphore_wait(barrier, len(known))
    halo = [
        pltpu.make_async_remote_copy(
            src_ref=out.at[i], dst_ref=got.at[1 - i], send_sem=halo_send.at[i], recv_sem=halo_recv.at[1 - i],
            device_id=device, device_id_type=MESH,
        )
        for i, device in enumerate((left, right))
    ]
    for copy in halo:
        copy.start()
    constants[1].wait()
    high[...] = matrix[...].astype(jnp.bfloat16)
    low[...] = (matrix[...] - high[...].astype(jnp.float32)).astype(jnp.bfloat16)

    def solve(p, carry):
        block = v[p]
        delta = pltpu.roll(block, points - 1, 0) - pltpu.roll(block, 1, 0)
        coarse = delta.astype(jnp.bfloat16)
        fine = (delta - coarse.astype(jnp.float32)).astype(jnp.bfloat16)
        local = (
            jnp.dot(low[...], coarse, preferred_element_type=jnp.float32)
            + jnp.dot(high[...], fine, preferred_element_type=jnp.float32)
        ) + jnp.dot(high[...], coarse, preferred_element_type=jnp.float32)
        d_ref[p] = local
        one = pl.ds(p, 1)
        rows[2, one, :] = local[0:1]
        rows[3, one, :] = local[points - 1 :]
        rows[4, one, :] = column_sum(columns[0], local[:REACH])
        rows[5, one, :] = column_sum(columns[1], local[points - REACH :])
        rows[6, one, :] = jnp.sum(local * local, axis=0, keepdims=True)
        return carry

    lax.fori_loop(0, planes, solve, 0)

    for copy in halo:
        copy.wait()

    energy = rows[6]
    squares = 1.0 / (1.0 - ROOT * ROOT)
    for side, sign in ((0, 1.0), (1, -1.0)):
        own, inner, edge = out[side, 0], rows[side], got[side, 0]
        jump = sign * (inner - edge)
        total = jump + got[side, 1] + (sign * ROOT) * (own - edge)
        energy = energy + 2.0 * (TAIL * total * rows[4 + side] + BUMP * jump * rows[2 + side])
        energy = energy + (TAIL * TAIL * squares) * total * total
        energy = energy + (2.0 * TAIL * BUMP) * total * jump + (BUMP * BUMP) * jump * jump
        tots[side] = TAIL * total
        tots[2 + side] = BUMP * jump

    energy = jnp.sum(energy[:, :LANES] + energy[:, LANES:], axis=1, keepdims=True)
    chosen = lax.broadcasted_iota(jnp.int32, (planes, LANES), 0) == lax.broadcasted_iota(jnp.int32, (planes, LANES), 1)
    share = jnp.sum(jnp.where(chosen, jnp.broadcast_to(energy, (planes, LANES)), 0.0), axis=0, keepdims=True)

    def send_sums(phase, group):
        n = len(group)
        for i, device in enumerate(group):
            pltpu.make_async_remote_copy(
                src_ref=shares.at[phase, pl.ds(n, 1)], dst_ref=shares.at[phase, pl.ds(i, 1)],
                send_sem=sum_send.at[phase], recv_sem=sum_recv.at[phase],
                device_id=device, device_id_type=MESH,
            ).start()

    def all_of(phase, group, semaphore):
        part = shares.at[phase, pl.ds(0, len(group))]
        return pltpu.make_async_copy(part, part, semaphore.at[phase])

    shares[0, len(groups[0]) : len(groups[0]) + 1, :] = share
    send_sums(0, groups[0])

    def correct(p, carry):
        one = pl.ds(p, 1)
        for side in range(2):
            wide = jnp.concatenate([columns[side], columns[side]], axis=1)
            place = pl.ds(0, REACH) if side == 0 else pl.ds(points - REACH, REACH)
            d_ref[p, place, :] = d_ref[p, place, :] + wide * tots[side, one, :]
        top, bottom = pl.ds(0, 1), pl.ds(points - 1, 1)
        d_ref[p, top, :] = d_ref[p, top, :] + tots[2, one, :]
        d_ref[p, bottom, :] = d_ref[p, bottom, :] + tots[3, one, :]
        return carry

    lax.fori_loop(0, planes, correct, 0)

    all_of(0, groups[0], sum_recv).wait()
    share = jnp.sum(shares[0], axis=0, keepdims=True)
    shares[1, len(groups[1]) : len(groups[1]) + 1, :] = share
    send_sums(1, groups[1])
    all_of(1, groups[1], sum_recv).wait()
    total = jnp.sum(shares[1], axis=0, keepdims=True)
    count = float(points * ring * 2 * LANES * lax.axis_size("gz"))
    e_ref[...] = total * (1.0 / count)
    all_of(0, groups[0], sum_send).wait()
    all_of(1, groups[1], sum_send).wait()


def shards(velocity):
    components, heights, points, spanwise = velocity.shape
    planes = components * heights
    matrix, columns = tables(points)
    whole = pl.BlockSpec(memory_space=pltpu.HBM)
    derivative, energy = pl.pallas_call(
        functools.partial(kernel, planes, points),
        out_shape=(
            pltpu.VMEM((planes, points, spanwise), jnp.float32),
            jax.ShapeDtypeStruct((1, LANES), jnp.float32),
        ),
        in_specs=[whole] * 3,
        out_specs=(pl.BlockSpec(memory_space=pltpu.VMEM), pl.BlockSpec(memory_space=pltpu.VMEM)),
        scratch_shapes=[
            pltpu.VMEM((planes, points, spanwise), jnp.float32),
            pltpu.VMEM((points, points), jnp.float32),
            pltpu.VMEM((points, points), jnp.bfloat16),
            pltpu.VMEM((points, points), jnp.bfloat16),
            pltpu.VMEM((4, REACH, LANES), jnp.float32),
            pltpu.VMEM((2, 2, planes, spanwise), jnp.float32),
            pltpu.VMEM((2, 2, planes, spanwise), jnp.float32),
            pltpu.VMEM((7, planes, spanwise), jnp.float32),
            pltpu.VMEM((4, planes, spanwise), jnp.float32),
            pltpu.VMEM((2, 16, LANES), jnp.float32),
            pltpu.SemaphoreType.DMA((planes,)),
            pltpu.SemaphoreType.DMA((2,)),
            pltpu.SemaphoreType.DMA((2,)),
            pltpu.SemaphoreType.DMA((2,)),
            pltpu.SemaphoreType.DMA((2,)),
            pltpu.SemaphoreType.DMA((2,)),
        ],
        compiler_params=pltpu.CompilerParams(
            collective_id=0, has_side_effects=True, vmem_limit_bytes=24 * 1024 * 1024
        ),
        name="derive",
    )(*(
        pltpu.with_memory_space_constraint(operand, pltpu.HBM)
        for operand in (velocity.reshape(planes, points, spanwise), jnp.asarray(matrix), jnp.asarray(columns))
    ))
    return (
        derivative.reshape(velocity.shape),
        energy[0, :planes].reshape(components, heights),
    )


def solution(mesh):
    return jax.shard_map(
        shards,
        mesh=mesh,
        in_specs=(P(None, None, "gx", "gz"),),
        out_specs=(P(None, None, "gx", "gz"), P()),
        check_vma=False,
    )
```

time: 117 us -> 33.7 us (0.29)
  blocking collectives: 76.3 us -> 0 us
  Pallas kernels: 0 us -> 29.6 us
  starting transfers between devices: 11.7 us -> 0 us
  matrix products: 9.82 us -> 0 us
  waiting for transfers between devices: 5.96 us -> 0 us
  other arithmetic: 5.54 us -> 0 us
  between operations: 2.7 us -> 0.64 us
  local copies, waits for them, and re-layouts: 5.03 us -> 3.39 us
    psum x1 -> x0, blocking collectives: 76.3 us -> none  [shards(): totals = lax.psum(local_sums, ('gx', 'gz'))]
    pallas_call x0 -> x1, Pallas kernels: none -> 29.6 us  [shards(): pl.pallas_call(functools.partial(kernel, planes, points), out_shape=(pltp...]
    ppermute x4 -> x0, starting transfers between devices: 11.7 us -> none  [the longest x1 6.84 us: padded_2(): lax.ppermute(head, axis, [((i + 1) % count, i) for i in range(count)])]
    dot_general x1 -> x0, matrix products: 9.82 us -> none  [edge_solve(): jnp.einsum('ij,cpjz->cpiz', inverse, right_side, precision=lax.Precision....]
    ppermute x4 -> x0, waiting for transfers between devices: 5.96 us -> none  [the longest x2 5.95 us: shifted(): return lax.ppermute(block, axis, route)]
    reduce_sum x1 -> x0, other arithmetic: 4.38 us -> none  [shards(): local_sums = jnp.sum(derivative * derivative, axis=(2, 3))]
    slice x4 -> x1, local copies, waits for them, and re-layouts: 1.61 us -> 0.02 us  [shards(): energy[0, :planes].reshape(components, heights)]
    unnamed x7 -> x1, local copies, waits for them, and re-layouts: 3.39 us -> 2.71 us
  transfers between devices with their start and end apart: 4 -> 0, of which waited for: 1 -> 0; matrix products, arithmetic and copies ran while one was open for 4% -> 0% of each run, Pallas kernels for 0% -> 0%
where the time goes in v1:
time: 33.7 us
  Pallas kernels  29.6 us (88%)
  local copies, waits for them, and re-layouts  3.39 us (10%)
  between operations  0.64 us (2%)
    pallas_call x1, Pallas kernels, shards(): pl.pallas_call(functools.partial(kernel, planes, points), out_shape=(pltp...  29.6 us
    unnamed x1, local copies, waits for them, and re-layouts  2.71 us

profile of v1, /device:TPU:1, one launch (start us, length us, event | category | flops | bytes accessed | tf_op | source)
XLA Modules:
  0.0 33.7 jit_solution(1931718432351790888)
XLA Ops:
  0.6 29.6 %derive.1 = (f32[24,256,256]{2,1,0:T(8,128)S(1)}, f32[1,128]{1,0:T(1,128)S(1)}) custom-call(f32[24,256,256]{2,1,0:T(8,128)} %bitcast.3, f32[256,256]{1,0:T(8,128)} %constant.4.clone.matrix_hbm, f32[4,96,128]{2,1,0:T(8,128)} %constant.5.clone.column_hbm), custom_call_target="tpu_custom_call" | custom-call | tf_op jit(solution)/shard_map/derive/pallas_call | solution.py:214
  30.3 2.7 %copy.6 = f32[3,8,256,256]{3,2,1,0:T(8,128)} copy(f32[3,8,256,256]{3,2,1,0:T(8,128)S(1)} %bitcast.2) | data formatting | bytes 12582912
  33.0 0.7 %reshape_squeeze.3 = f32[3,8]{1,0:T(4,128)} reshape(f32[24]{0:T(128)S(1)} %slice_reduce_fusion) | data formatting | bytes 192 | tf_op jit(solution)/shard_map/reshape;squeeze | solution.py:250
  (1 shorter events, 0.0 us)

commit v2 on v1

--- a/solution.py
+++ b/solution.py
@@ -25,6 +25,8 @@
 PHASES = (("x", "y"), ("z", "core"))
 MESH = pl.DeviceIdType.MESH
 LANES = 128
+PIECE = 4
+GROUP = 8
 
 
 def hops(offset, axis):
@@ -68,7 +70,7 @@
 
 def kernel(
     planes, points, v_hbm, matrix_hbm, column_hbm, d_ref, e_ref,
-    v, matrix, high, low, columns, out, got, rows, tots, shares, load_sem, const_sem, halo_send, halo_recv, sum_send, sum_recv,
+    v, matrix, split, columns, out, got, rows, tots, shares, load_sem, const_sem, halo_send, halo_recv, sum_send, sum_recv,
 ):
     gx, gz = lax.axis_index("gx"), lax.axis_index("gz")
     ring = lax.axis_size("gx")
@@ -85,17 +87,17 @@
         for i, (source, target) in enumerate(((column_hbm, columns), (matrix_hbm, matrix)))
     ]
 
-    def load(p):
-        return pltpu.make_async_copy(v_hbm.at[p], v.at[p], load_sem.at[p])
+    def load(i):
+        part = pl.ds(i * PIECE, PIECE)
+        return pltpu.make_async_copy(v_hbm.at[part], v.at[part], load_sem.at[i])
 
     constants[0].start()
-    for p in range(planes):
-        load(p).start()
+    for i in range(planes // PIECE):
+        load(i).start()
     constants[1].start()
     constants[0].wait()
 
-    def summarise(p, carry):
-        load(p).wait()
+    def summarise(p):
         head, tail = v[p, :REACH, :], v[p, points - REACH :, :]
         first, second = head[0:1], head[1:2]
         last, before = tail[REACH - 1 :], tail[REACH - 2 : REACH - 1]
@@ -108,9 +110,14 @@
         out[1, 1, one, :] = column_sum(columns[3], tail) + ROOT * (last - before)
         rows[0, one, :] = second
         rows[1, one, :] = before
+
+    def summarise_piece(i, carry):
+        load(i).wait()
+        for k in range(PIECE):
+            summarise(i * PIECE + k)
         return carry
 
-    lax.fori_loop(0, planes, summarise, 0)
+    lax.fori_loop(0, planes // PIECE, summarise_piece, 0)
 
     pl.semaphore_wait(barrier, len(known))
     halo = [
@@ -123,18 +130,19 @@
     for copy in halo:
         copy.start()
     constants[1].wait()
-    high[...] = matrix[...].astype(jnp.bfloat16)
-    low[...] = (matrix[...] - high[...].astype(jnp.float32)).astype(jnp.bfloat16)
-
-    def solve(p, carry):
+    high = matrix[...].astype(jnp.bfloat16)
+    split[:, :points] = (matrix[...] - high.astype(jnp.float32)).astype(jnp.bfloat16)
+    split[:, points : 2 * points] = high
+    split[:, 2 * points :] = high
+
+    def solve(p):
         block = v[p]
         delta = pltpu.roll(block, points - 1, 0) - pltpu.roll(block, 1, 0)
         coarse = delta.astype(jnp.bfloat16)
         fine = (delta - coarse.astype(jnp.float32)).astype(jnp.bfloat16)
-        local = (
-            jnp.dot(low[...], coarse, preferred_element_type=jnp.float32)
-            + jnp.dot(high[...], fine, preferred_element_type=jnp.float32)
-        ) + jnp.dot(high[...], coarse, preferred_element_type=jnp.float32)
+        local = jnp.dot(
+            split[...], jnp.concatenate([coarse, fine, coarse], axis=0), preferred_element_type=jnp.float32
+        )
         d_ref[p] = local
         one = pl.ds(p, 1)
         rows[2, one, :] = local[0:1]
@@ -142,9 +150,13 @@
         rows[4, one, :] = column_sum(columns[0], local[:REACH])
         rows[5, one, :] = column_sum(columns[1], local[points - REACH :])
         rows[6, one, :] = jnp.sum(local * local, axis=0, keepdims=True)
+
+    def solve_group(i, carry):
+        for k in range(GROUP):
+            solve(i * GROUP + k)
         return carry
 
-    lax.fori_loop(0, planes, solve, 0)
+    lax.fori_loop(0, planes // GROUP, solve_group, 0)
 
     for copy in halo:
         copy.wait()
@@ -201,9 +213,19 @@
     all_of(1, groups[1], sum_recv).wait()
     total = jnp.sum(shares[1], axis=0, keepdims=True)
     count = float(points * ring * 2 * LANES * lax.axis_size("gz"))
-    e_ref[...] = total * (1.0 / count)
+    total = total * (1.0 / count)
+    per_row = e_ref.shape[1]
+    for i in range(e_ref.shape[0]):
+        e_ref[i : i + 1, :] = total[:, i * per_row : (i + 1) * per_row]
     all_of(0, groups[0], sum_send).wait()
     all_of(1, groups[1], sum_send).wait()
+
+
+def deliver(d_vmem, e_vmem, d_hbm, e_ref, sem):
+    copy = pltpu.make_async_copy(d_vmem, d_hbm, sem)
+    copy.start()
+    e_ref[...] = e_vmem[...]
+    copy.wait()
 
 
 def shards(velocity):
@@ -215,22 +237,21 @@
         functools.partial(kernel, planes, points),
         out_shape=(
             pltpu.VMEM((planes, points, spanwise), jnp.float32),
-            jax.ShapeDtypeStruct((1, LANES), jnp.float32),
+            pltpu.VMEM((components, heights), jnp.float32),
         ),
         in_specs=[whole] * 3,
         out_specs=(pl.BlockSpec(memory_space=pltpu.VMEM), pl.BlockSpec(memory_space=pltpu.VMEM)),
         scratch_shapes=[
             pltpu.VMEM((planes, points, spanwise), jnp.float32),
             pltpu.VMEM((points, points), jnp.float32),
-            pltpu.VMEM((points, points), jnp.bfloat16),
-            pltpu.VMEM((points, points), jnp.bfloat16),
+            pltpu.VMEM((points, 3 * points), jnp.bfloat16),
             pltpu.VMEM((4, REACH, LANES), jnp.float32),
             pltpu.VMEM((2, 2, planes, spanwise), jnp.float32),
             pltpu.VMEM((2, 2, planes, spanwise), jnp.float32),
             pltpu.VMEM((7, planes, spanwise), jnp.float32),
             pltpu.VMEM((4, planes, spanwise), jnp.float32),
             pltpu.VMEM((2, 16, LANES), jnp.float32),
-            pltpu.SemaphoreType.DMA((planes,)),
+            pltpu.SemaphoreType.DMA((planes // PIECE,)),
             pltpu.SemaphoreType.DMA((2,)),
             pltpu.SemaphoreType.DMA((2,)),
             pltpu.SemaphoreType.DMA((2,)),
@@ -245,10 +266,19 @@
         pltpu.with_memory_space_constraint(operand, pltpu.HBM)
         for operand in (velocity.reshape(planes, points, spanwise), jnp.asarray(matrix), jnp.asarray(columns))
     ))
-    return (
-        derivative.reshape(velocity.shape),
-        energy[0, :planes].reshape(components, heights),
-    )
+    derivative, energy = pl.pallas_call(
+        deliver,
+        out_shape=(
+            jax.ShapeDtypeStruct(derivative.shape, jnp.float32),
+            jax.ShapeDtypeStruct(energy.shape, jnp.float32),
+        ),
+        in_specs=[pl.BlockSpec(memory_space=pltpu.VMEM)] * 2,
+        out_specs=(whole, pl.BlockSpec(memory_space=pltpu.VMEM)),
+        scratch_shapes=[pltpu.SemaphoreType.DMA],
+        compiler_params=pltpu.CompilerParams(vmem_limit_bytes=4 * 1024 * 1024),
+        name="deliver",
+    )(derivative, energy)
+    return derivative.reshape(velocity.shape), energy
 
 
 def solution(mesh):

time: 33.7 us -> 28.2 us (0.84)
  local copies, waits for them, and re-layouts: 3.39 us -> 0 us
  Pallas kernels: 29.6 us -> 27.5 us
    pallas_call x1, Pallas kernels: 29.6 us -> 24.2 us  [shards(): pl.pallas_call(functools.partial(kernel, planes, points), out_shape=(pltp...]
    pallas_call x0 -> x1, Pallas kernels: none -> 3.29 us  [shards(): pl.pallas_call(deliver, out_shape=(jax.ShapeDtypeStruct(derivative.shape,...]
    unnamed x1 -> x0, local copies, waits for them, and re-layouts: 2.71 us -> none
    another operation x1 -> x0, local copies, waits for them, and re-layouts: 0.66 us -> none  [shards(): energy[0, :planes].reshape(components, heights)]
where the time goes in v2:
time: 28.2 us; the launch traced here: 28.1 us
  Pallas kernels  27.5 us (98%)
  between operations  0.64 us (2%)
    pallas_call x1, Pallas kernels, shards(): pl.pallas_call(functools.partial(kernel, planes, points), out_shape=(pltp...  24.2 us
    pallas_call x1, Pallas kernels, shards(): pl.pallas_call(deliver, out_shape=(jax.ShapeDtypeStruct(derivative.shape,...  3.29 us

profile of v2, /device:TPU:1, one launch (start us, length us, event | category | flops | bytes accessed | tf_op | source)
XLA Modules:
  0.0 28.1 jit_solution(1266905641361109030)
XLA Ops:
  0.6 24.2 %derive.1 = (f32[24,256,256]{2,1,0:T(8,128)S(1)}, f32[3,8]{1,0:T(4,128)S(1)}) custom-call(f32[24,256,256]{2,1,0:T(8,128)} %bitcast.2, f32[256,256]{1,0:T(8,128)} %constant.4.clone.matrix_hbm, f32[4,96,128]{2,1,0:T(8,128)} %constant.5.clone.column_hbm), custom_call_target="tpu_custom_call" | custom-call | tf_op jit(solution)/shard_map/derive/pallas_call | solution.py:236
  24.8 3.3 %deliver.1 = (f32[24,256,256]{2,1,0:T(8,128)}, f32[3,8]{1,0:T(4,128)}) custom-call(f32[24,256,256]{2,1,0:T(8,128)S(1)} %get-tuple-element.6.d_vmem, f32[3,8]{1,0:T(4,128)S(1)} %get-tuple-element.7.e_vmem), custom_call_target="tpu_custom_call" | custom-call | tf_op jit(solution)/shard_map/deliver/pallas_call | solution.py:269

commit v3 on v2

v3 whole, which is shorter than its diff:
```python
import functools
import itertools
import math

import jax
import jax.numpy as jnp
import numpy as np
from jax import lax
from jax.experimental import pallas as pl
from jax.experimental.pallas import tpu as pltpu
from jax.sharding import PartitionSpec as P

ALPHA = 1.0 / 3.0
HALF_A = 7.0 / 9.0
QUARTER_B = 1.0 / 36.0

ROOT = (math.sqrt(1.0 - 4.0 * ALPHA * ALPHA) - 1.0) / (2.0 * ALPHA)
SCALE = 1.0 / math.sqrt(1.0 - 4.0 * ALPHA * ALPHA)
TAIL = SCALE * (HALF_A + QUARTER_B * (ROOT + 1.0 / ROOT))
CENTRE = SCALE * (HALF_A + 2.0 * QUARTER_B * ROOT)
BUMP = CENTRE - TAIL
REACH = 96

SIZES = {"x": 4, "y": 4, "z": 8, "core": 2}
PHASES = (("x", "y"), ("z", "core"))
AHEAD = {"x": 0, "y": 0, "z": 0, "core": 1}
FAR = range(3, 8)
MESH = pl.DeviceIdType.MESH
LANES = 128
ROW = SIZES["x"] * SIZES["core"]
PIECE = 4
GROUP = 8
MIB = 1024 * 1024


def around():
    gx, gz = lax.axis_index("gx"), lax.axis_index("gz")
    here = {"z": lax.div(gx, 4), "y": lax.rem(gx, 4), "x": lax.div(gz, 2), "core": lax.rem(gz, 2)}

    @functools.cache
    def moved(axis, offset):
        return lax.rem(here[axis] + offset, SIZES[axis]) if offset else here[axis]

    @functools.cache
    def paired(major, minor, one, two):
        if not (one or two):
            return gx if major == "z" else gz
        return moved(major, one) * SIZES[minor] + moved(minor, two)

    def at(x=0, y=0, z=0, core=0):
        return (
            paired("z", "y", z % SIZES["z"], y % SIZES["y"]),
            paired("x", "core", x % SIZES["x"], core % SIZES["core"]),
        )

    return at


def hops(offset, axis):
    return 0 if axis == "core" else min(offset, SIZES[axis] - offset)


def partners(at, axes):
    offsets = [o for o in itertools.product(*(range(SIZES[a]) for a in axes)) if any(o)]
    offsets.sort(key=lambda o: -sum(hops(v, a) for v, a in zip(o, axes)))
    return [at(**dict(zip(axes, offset))) for offset in offsets]


def far_devices():
    found = []
    for z, y, x, core in itertools.product(FAR, *(range(SIZES[a]) for a in ("y", "x", "core"))):
        place = {"x": x, "y": y, "z": z, "core": core}
        away = sum(hops(abs(place[a] - AHEAD[a]), a) for a in place)
        found.append((-away, z * SIZES["y"] + y, x * SIZES["core"] + core))
    return [there for _, *there in sorted(found)]


def tables(points):
    index = np.arange(points)
    distance = np.abs(index[:, None] - index[None, :])
    matrix = np.where(distance == 0, CENTRE, TAIL * ROOT ** distance.astype(np.float64))
    matrix[:, 0] = 0.0
    matrix[:, points - 1] = 0.0
    reach = np.arange(REACH)
    powers = ROOT ** reach.astype(np.float64)
    head = ROOT ** (reach + 1.0)
    head[0] = head[REACH - 1] = 0.0
    columns = np.stack([powers, powers[::-1], head, head[::-1]])
    columns = np.broadcast_to(columns[:, :, None], (4, REACH, LANES))
    return matrix.astype(np.float32), columns.astype(np.float32)


def column_sum(weights, block):
    w = jnp.concatenate([weights, weights], axis=1)
    return jnp.sum(w * block, axis=0, keepdims=True)


def derive(
    v_hbm, matrix_hbm, column_hbm, d_ref, e_ref,
    v, matrix, split, columns, out, got, rows, tots, shares, load_sem, const_sem, halo_send, halo_recv, sum_send, sum_recv,
    direct, extra, direct_send, direct_recv,
):
    planes, points, _ = v.shape
    parts, per_part = out.shape[1], out.shape[3]
    gx, gz = lax.axis_index("gx"), lax.axis_index("gz")
    ring = lax.axis_size("gx")
    sides = ((lax.rem(gx + ring - 1, ring), gz), (lax.rem(gx + 1, ring), gz))

    at = around()
    groups = [partners(at, axes) for axes in PHASES]

    shares[1] = jnp.zeros_like(shares[1])
    extra[...] = jnp.zeros_like(extra)

    constants = [
        pltpu.make_async_copy(source, target, const_sem.at[i])
        for i, (source, target) in enumerate(((column_hbm, columns), (matrix_hbm, matrix)))
    ]

    def load(i):
        piece = pl.ds(i * PIECE, PIECE)
        return pltpu.make_async_copy(v_hbm.at[piece], v.at[piece], load_sem.at[i])

    constants[0].start()
    for i in range(planes // PIECE):
        load(i).start()
    constants[1].start()

    def signal(semaphore, there):
        pl.semaphore_signal(semaphore, inc=1, device_id=there, device_id_type=MESH)

    barrier = pltpu.get_barrier_semaphore()
    known = groups[1] + groups[0] + list(sides)
    for there in known:
        signal(barrier, there)

    first = (AHEAD["z"] * SIZES["y"] + AHEAD["y"], AHEAD["x"] * SIZES["core"] + AHEAD["core"])
    is_first = (gx == first[0]) & (gz == first[1])
    low, high_end = FAR.start * SIZES["y"], FAR.stop * SIZES["y"]
    is_far = (gx >= low) & (gx < high_end)

    @pl.when(is_first)
    def _():
        for there in far_devices():
            signal(barrier, there)

    constants[0].wait()

    def summarise(part, k):
        p = part * per_part + k
        head, tail = v[p, :REACH, :], v[p, points - REACH :, :]
        first, second = head[0:1], head[1:2]
        last, before = tail[REACH - 1 :], tail[REACH - 2 : REACH - 1]
        head = pltpu.roll(head, REACH - 1, 0) - pltpu.roll(head, 1, 0)
        tail = pltpu.roll(tail, REACH - 1, 0) - pltpu.roll(tail, 1, 0)
        one, row = pl.ds(p, 1), pl.ds(k, 1)
        out[0, part, 0, row, :] = first
        out[0, part, 1, row, :] = column_sum(columns[2], head) + ROOT * (second - first)
        out[1, part, 0, row, :] = last
        out[1, part, 1, row, :] = column_sum(columns[3], tail) + ROOT * (last - before)
        rows[0, one, :] = second
        rows[1, one, :] = before

    def halo(part, i):
        return pltpu.make_async_remote_copy(
            src_ref=out.at[i, part], dst_ref=got.at[1 - i, part],
            send_sem=halo_send.at[i, part], recv_sem=halo_recv.at[1 - i, part],
            device_id=sides[i], device_id_type=MESH,
        )

    for part in range(parts):

        def summarise_piece(i, carry):
            load(part * (per_part // PIECE) + i).wait()
            for k in range(PIECE):
                summarise(part, i * PIECE + k)
            return carry

        lax.fori_loop(0, per_part // PIECE, summarise_piece, 0)

    pl.semaphore_wait(barrier, len(known) + is_far.astype(jnp.int32))
    for part in range(parts):
        for i in range(2):
            halo(part, i).start()
    constants[1].wait()
    high = matrix[...].astype(jnp.bfloat16)
    split[:, :points] = (matrix[...] - high.astype(jnp.float32)).astype(jnp.bfloat16)
    split[:, points : 2 * points] = high
    split[:, 2 * points :] = high
    def solve(p):
        block = v[p]
        delta = pltpu.roll(block, points - 1, 0) - pltpu.roll(block, 1, 0)
        coarse = delta.astype(jnp.bfloat16)
        fine = (delta - coarse.astype(jnp.float32)).astype(jnp.bfloat16)
        local = jnp.dot(
            split[...], jnp.concatenate([coarse, fine, coarse], axis=0), preferred_element_type=jnp.float32
        )
        d_ref[p] = local
        one = pl.ds(p, 1)
        rows[2, one, :] = local[0:1]
        rows[3, one, :] = local[points - 1 :]
        rows[4, one, :] = column_sum(columns[0], local[:REACH])
        rows[5, one, :] = column_sum(columns[1], local[points - REACH :])
        rows[6, one, :] = jnp.sum(local * local, axis=0, keepdims=True)

    def solve_group(i, carry):
        for k in range(GROUP):
            solve(i * GROUP + k)
        return carry

    lax.fori_loop(0, planes // GROUP, solve_group, 0)

    squares = 1.0 / (1.0 - ROOT * ROOT)
    sums = []
    for part in range(parts):
        span = pl.ds(part * per_part, per_part)
        energy = rows[6, span, :]
        for i in range(2):
            halo(part, i).wait()
        for side, sign in ((0, 1.0), (1, -1.0)):
            own, inner, edge = out[side, part, 0], rows[side, span, :], got[side, part, 0]
            jump = sign * (inner - edge)
            total = jump + got[side, part, 1] + (sign * ROOT) * (own - edge)
            energy = energy + 2.0 * (TAIL * total * rows[4 + side, span, :] + BUMP * jump * rows[2 + side, span, :])
            energy = energy + (TAIL * TAIL * squares) * total * total
            energy = energy + (2.0 * TAIL * BUMP) * total * jump + (BUMP * BUMP) * jump * jump
            tots[side, span, :] = TAIL * total
            tots[2 + side, span, :] = BUMP * jump
        sums.append(jnp.sum(energy[:, :LANES] + energy[:, LANES:], axis=1, keepdims=True))

    chosen = lax.broadcasted_iota(jnp.int32, (planes, LANES), 0) == lax.broadcasted_iota(jnp.int32, (planes, LANES), 1)
    energy = jnp.broadcast_to(jnp.concatenate(sums, axis=0), (planes, LANES))
    share = jnp.sum(jnp.where(chosen, energy, 0.0), axis=0, keepdims=True)

    n_far = direct.shape[0]

    def send_direct():
        return pltpu.make_async_remote_copy(
            src_ref=shares.at[0, pl.ds(len(groups[0]), 1)], dst_ref=direct.at[pl.ds((gx - low) * ROW + gz, 1)],
            send_sem=direct_send, recv_sem=direct_recv, device_id=first, device_id_type=MESH,
        )

    def send_sum(phase, i):
        group = groups[phase]
        return pltpu.make_async_remote_copy(
            src_ref=shares.at[phase, pl.ds(len(group), 1)], dst_ref=shares.at[phase, pl.ds(i, 1)],
            send_sem=sum_send.at[phase], recv_sem=sum_recv.at[phase],
            device_id=group[i], device_id_type=MESH,
        )

    def rows_of(phase, count, semaphore):
        part = shares.at[phase, pl.ds(0, count)]
        return pltpu.make_async_copy(part, part, semaphore.at[phase])

    n_near, n_level = len(groups[0]), len(groups[1])
    skips = is_far & (lax.rem(gx, SIZES["y"]) == AHEAD["y"]) & (lax.div(gz, SIZES["core"]) == AHEAD["x"])
    n_skip = len(FAR) * SIZES["core"]

    shares[0, n_near : n_near + 1, :] = share

    @pl.when(is_far)
    def _():
        send_direct().start()

    for i in range(n_near):
        send_sum(0, i).start()

    def correct(p, carry):
        one = pl.ds(p, 1)
        for side in range(2):
            wide = jnp.concatenate([columns[side], columns[side]], axis=1)
            place = pl.ds(0, REACH) if side == 0 else pl.ds(points - REACH, REACH)
            d_ref[p, place, :] = d_ref[p, place, :] + wide * tots[side, one, :]
        top, bottom = pl.ds(0, 1), pl.ds(points - 1, 1)
        d_ref[p, top, :] = d_ref[p, top, :] + tots[2, one, :]
        d_ref[p, bottom, :] = d_ref[p, bottom, :] + tots[3, one, :]
        return carry

    lax.fori_loop(0, planes, correct, 0)

    rows_of(0, n_near, sum_recv).wait()
    shares[1, n_level : n_level + 1, :] = jnp.sum(shares[0], axis=0, keepdims=True)
    for i, there in enumerate(groups[1]):

        @pl.when(jnp.logical_not(skips & (there[0] == first[0]) & (there[1] == first[1])))
        def _(i=i):
            send_sum(1, i).start()

    @pl.when(is_first)
    def _():
        rows_of(1, n_level - n_skip, sum_recv).wait()
        pltpu.make_async_copy(direct, direct, direct_recv).wait()
        extra[...] = jnp.sum(direct[...], axis=0, keepdims=True)

    @pl.when(jnp.logical_not(is_first))
    def _():
        rows_of(1, n_level, sum_recv).wait()

    total = jnp.sum(shares[1], axis=0, keepdims=True) + extra[...]
    count = float(points * ring * 2 * LANES * lax.axis_size("gz"))
    total = total * (1.0 / count)
    per_row = e_ref.shape[1]
    for i in range(e_ref.shape[0]):
        e_ref[i : i + 1, :] = total[:, i * per_row : (i + 1) * per_row]
    rows_of(0, n_near, sum_send).wait()

    @pl.when(skips)
    def _():
        rows_of(1, n_level - 1, sum_send).wait()

    @pl.when(jnp.logical_not(skips))
    def _():
        rows_of(1, n_level, sum_send).wait()

    @pl.when(is_far)
    def _():
        send_direct().wait_send()


def deliver(d_vmem, e_vmem, d_hbm, e_hbm, sem):
    copies = [pltpu.make_async_copy(d_vmem, d_hbm, sem.at[0]), pltpu.make_async_copy(e_vmem, e_hbm, sem.at[1])]
    for copy in copies:
        copy.start()
    for copy in copies:
        copy.wait()


def shards(velocity):
    components, heights, points, spanwise = velocity.shape
    planes = components * heights
    shape = (planes, points, spanwise)
    matrix, columns = tables(points)
    f32, dma = jnp.float32, pltpu.SemaphoreType.DMA
    near, far = pl.BlockSpec(memory_space=pltpu.VMEM), pl.BlockSpec(memory_space=pltpu.HBM)
    halo = (2, components, 2, heights, spanwise)
    group = SIZES["x"] * SIZES["y"]

    derivative, energy = pl.pallas_call(
        derive,
        out_shape=(pltpu.VMEM(shape, f32), pltpu.VMEM((components, heights), f32)),
        in_specs=[far] * 3,
        out_specs=(near,) * 2,
        scratch_shapes=[
            pltpu.VMEM(shape, f32),
            pltpu.VMEM((points, points), f32),
            pltpu.VMEM((points, 3 * points), jnp.bfloat16),
            pltpu.VMEM(columns.shape, f32),
            pltpu.VMEM(halo, f32),
            pltpu.VMEM(halo, f32),
            pltpu.VMEM((7, planes, spanwise), f32),
            pltpu.VMEM((4, planes, spanwise), f32),
            pltpu.VMEM((2, group, LANES), f32),
            dma((planes // PIECE,)),
            dma((2,)),
            dma((2, components)),
            dma((2, components)),
            dma((2,)),
            dma((2,)),
            pltpu.VMEM((len(far_devices()), LANES), f32),
            pltpu.VMEM((1, LANES), f32),
            dma,
            dma,
        ],
        compiler_params=pltpu.CompilerParams(collective_id=0, has_side_effects=True, vmem_limit_bytes=24 * MIB),
        name="derive",
    )(*(
        pltpu.with_memory_space_constraint(operand, pltpu.HBM)
        for operand in (velocity.reshape(shape), jnp.asarray(matrix), jnp.asarray(columns))
    ))
    derivative, energy = pl.pallas_call(
        deliver,
        out_shape=(jax.ShapeDtypeStruct(shape, f32), jax.ShapeDtypeStruct((components, heights), f32)),
        in_specs=[near] * 2,
        out_specs=(far, far),
        scratch_shapes=[dma((2,))],
        compiler_params=pltpu.CompilerParams(vmem_limit_bytes=4 * MIB),
        name="deliver",
    )(derivative, energy)
    return derivative.reshape(velocity.shape), energy


def solution(mesh):
    return jax.shard_map(
        shards,
        mesh=mesh,
        in_specs=(P(None, None, "gx", "gz"),),
        out_specs=(P(None, None, "gx", "gz"), P()),
        check_vma=False,
    )
```

time: 28.2 us -> 26.3 us (0.933)
  the two profiles are of different devices: /device:TPU:1 before, /device:TPU:8 now
where the time goes in v3:
time: 26.3 us; the launch traced here: 26.2 us
  Pallas kernels  25.5 us (97%)
  between operations  0.64 us (2%)
    pallas_call x1, Pallas kernels, shards(): pl.pallas_call(derive, out_shape=(pltpu.VMEM(shape, f32), pltpu.VMEM((com...  22.8 us
    pallas_call x1, Pallas kernels, shards(): pl.pallas_call(deliver, out_shape=(jax.ShapeDtypeStruct(shape, f32), jax....  2.72 us

profile of v3, /device:TPU:8, one launch (start us, length us, event | category | flops | bytes accessed | tf_op | source)
XLA Modules:
  0.0 26.2 jit_solution(7042745671913228255)
XLA Ops:
  0.6 22.8 %derive.1 = (f32[24,256,256]{2,1,0:T(8,128)S(1)}, f32[3,8]{1,0:T(4,128)S(1)}) custom-call(f32[24,256,256]{2,1,0:T(8,128)} %bitcast.2, f32[256,256]{1,0:T(8,128)} %constant.4.clone.matrix_hbm, f32[4,96,128]{2,1,0:T(8,128)} %constant.5.clone.column_hbm), custom_call_target="tpu_custom_call" | custom-call | tf_op jit(solution)/shard_map/derive/pallas_call | solution.py:338
  23.4 2.7 %deliver.1 = (f32[24,256,256]{2,1,0:T(8,128)}, f32[3,8]{1,0:T(4,128)}) custom-call(f32[24,256,256]{2,1,0:T(8,128)S(1)} %get-tuple-element.6.d_vmem, f32[3,8]{1,0:T(4,128)S(1)} %get-tuple-element.7.e_vmem), custom_call_target="tpu_custom_call" | custom-call | tf_op jit(solution)/shard_map/deliver/pallas_call | solution.py:370

commit v4 on v3

--- a/solution.py
+++ b/solution.py
@@ -83,9 +83,9 @@
     matrix[:, points - 1] = 0.0
     reach = np.arange(REACH)
     powers = ROOT ** reach.astype(np.float64)
-    head = ROOT ** (reach + 1.0)
-    head[0] = head[REACH - 1] = 0.0
-    columns = np.stack([powers, powers[::-1], head, head[::-1]])
+    head = ROOT**reach - ROOT ** (reach + 2.0)
+    head[0], head[1] = 0.0, ROOT - ROOT**3
+    columns = np.stack([powers, powers[::-1], head, -head[::-1]])
     columns = np.broadcast_to(columns[:, :, None], (4, REACH, LANES))
     return matrix.astype(np.float32), columns.astype(np.float32)
 
@@ -98,7 +98,7 @@
 def derive(
     v_hbm, matrix_hbm, column_hbm, d_ref, e_ref,
     v, matrix, split, columns, out, got, rows, tots, shares, load_sem, const_sem, halo_send, halo_recv, sum_send, sum_recv,
-    direct, extra, direct_send, direct_recv,
+    direct, extra, direct_send, direct_recv, near_sem, mate_sem,
 ):
     planes, points, _ = v.shape
     parts, per_part = out.shape[1], out.shape[3]
@@ -130,7 +130,10 @@
         pl.semaphore_signal(semaphore, inc=1, device_id=there, device_id_type=MESH)
 
     barrier = pltpu.get_barrier_semaphore()
-    known = groups[1] + groups[0] + list(sides)
+    row, column = partners(at, ("x",)), partners(at, ("y",))
+    levels = [at(z=offset) for offset in (2, -2, 1, -1)]
+    mate = at(core=1)
+    known = list(sides) + levels + row + column + [mate]
     for there in known:
         signal(barrier, there)
 
@@ -151,13 +154,11 @@
         head, tail = v[p, :REACH, :], v[p, points - REACH :, :]
         first, second = head[0:1], head[1:2]
         last, before = tail[REACH - 1 :], tail[REACH - 2 : REACH - 1]
-        head = pltpu.roll(head, REACH - 1, 0) - pltpu.roll(head, 1, 0)
-        tail = pltpu.roll(tail, REACH - 1, 0) - pltpu.roll(tail, 1, 0)
         one, row = pl.ds(p, 1), pl.ds(k, 1)
         out[0, part, 0, row, :] = first
-        out[0, part, 1, row, :] = column_sum(columns[2], head) + ROOT * (second - first)
+        out[0, part, 1, row, :] = column_sum(columns[2], head - first)
         out[1, part, 0, row, :] = last
-        out[1, part, 1, row, :] = column_sum(columns[3], tail) + ROOT * (last - before)
+        out[1, part, 1, row, :] = column_sum(columns[3], tail - last)
         rows[0, one, :] = second
         rows[1, one, :] = before
 
@@ -182,6 +183,9 @@
     for part in range(parts):
         for i in range(2):
             halo(part, i).start()
+    for there in row + levels[:2]:
+        signal(near_sem, there)
+
     constants[1].wait()
     high = matrix[...].astype(jnp.bfloat16)
     split[:, :points] = (matrix[...] - high.astype(jnp.float32)).astype(jnp.bfloat16)
@@ -262,8 +266,11 @@
     def _():
         send_direct().start()
 
+    pl.semaphore_wait(near_sem, len(row) + 2)
     for i in range(n_near):
         send_sum(0, i).start()
+
+    signal(mate_sem, mate)
 
     def correct(p, carry):
         one = pl.ds(p, 1)
@@ -280,6 +287,7 @@
 
     rows_of(0, n_near, sum_recv).wait()
     shares[1, n_level : n_level + 1, :] = jnp.sum(shares[0], axis=0, keepdims=True)
+    pl.semaphore_wait(mate_sem, 1)
     for i, there in enumerate(groups[1]):
 
         @pl.when(jnp.logical_not(skips & (there[0] == first[0]) & (there[1] == first[1])))
@@ -360,6 +368,8 @@
             pltpu.VMEM((1, LANES), f32),
             dma,
             dma,
+            pltpu.SemaphoreType.REGULAR,
+            pltpu.SemaphoreType.REGULAR,
         ],
         compiler_params=pltpu.CompilerParams(collective_id=0, has_side_effects=True, vmem_limit_bytes=24 * MIB),
         name="derive",

time: 26.3 us -> 25.5 us (0.970)
  the two profiles are of different devices: /device:TPU:8 before, /device:TPU:1 now
where the time goes in v4:
time: 25.5 us; the launch traced here: 25.1 us
  Pallas kernels  24.4 us (96%)
  between operations  0.64 us (3%)
    pallas_call x1, Pallas kernels, shards(): pl.pallas_call(derive, out_shape=(pltpu.VMEM(shape, f32), pltpu.VMEM((com...  21.7 us
    pallas_call x1, Pallas kernels, shards(): pl.pallas_call(deliver, out_shape=(jax.ShapeDtypeStruct(shape, f32), jax....  2.72 us

profile of v4, /device:TPU:1, one launch (start us, length us, event | category | flops | bytes accessed | tf_op | source)
XLA Modules:
  0.0 25.1 jit_solution(15103297974947553232)
XLA Ops:
  0.6 21.7 %derive.1 = (f32[24,256,256]{2,1,0:T(8,128)S(1)}, f32[3,8]{1,0:T(4,128)S(1)}) custom-call(f32[24,256,256]{2,1,0:T(8,128)} %bitcast.2, f32[256,256]{1,0:T(8,128)} %constant.4.clone.matrix_hbm, f32[4,96,128]{2,1,0:T(8,128)} %constant.5.clone.column_hbm), custom_call_target="tpu_custom_call" | custom-call | tf_op jit(solution)/shard_map/derive/pallas_call | solution.py:346
  22.4 2.7 %deliver.1 = (f32[24,256,256]{2,1,0:T(8,128)}, f32[3,8]{1,0:T(4,128)}) custom-call(f32[24,256,256]{2,1,0:T(8,128)S(1)} %get-tuple-element.6.d_vmem, f32[3,8]{1,0:T(4,128)S(1)} %get-tuple-element.7.e_vmem), custom_call_target="tpu_custom_call" | custom-call | tf_op jit(solution)/shard_map/deliver/pallas_call | solution.py:380

commit v5 on v4

--- a/solution.py
+++ b/solution.py
@@ -29,7 +29,7 @@
 LANES = 128
 ROW = SIZES["x"] * SIZES["core"]
 PIECE = 4
-GROUP = 8
+GROUP = 12
 MIB = 1024 * 1024
 
 
@@ -133,7 +133,7 @@
     row, column = partners(at, ("x",)), partners(at, ("y",))
     levels = [at(z=offset) for offset in (2, -2, 1, -1)]
     mate = at(core=1)
-    known = list(sides) + levels + row + column + [mate]
+    known = [*sides, *levels[:2], row[0], column[0], *levels[2:], *row[1:], *column[1:], mate]
     for there in known:
         signal(barrier, there)
 
@@ -178,11 +178,13 @@
             return carry
 
         lax.fori_loop(0, per_part // PIECE, summarise_piece, 0)
-
-    pl.semaphore_wait(barrier, len(known) + is_far.astype(jnp.int32))
-    for part in range(parts):
-        for i in range(2):
-            halo(part, i).start()
+        if part == parts - 2:
+            pl.semaphore_wait(barrier, len(known) + is_far.astype(jnp.int32))
+        if part >= parts - 2:
+            for ready in range(parts - 1) if part == parts - 2 else (part,):
+                for i in range(2):
+                    halo(ready, i).start()
+
     for there in row + levels[:2]:
         signal(near_sem, there)
 
@@ -288,11 +290,18 @@
     rows_of(0, n_near, sum_recv).wait()
     shares[1, n_level : n_level + 1, :] = jnp.sum(shares[0], axis=0, keepdims=True)
     pl.semaphore_wait(mate_sem, 1)
-    for i, there in enumerate(groups[1]):
-
-        @pl.when(jnp.logical_not(skips & (there[0] == first[0]) & (there[1] == first[1])))
-        def _(i=i):
+    @pl.when(jnp.logical_not(skips))
+    def _():
+        for i in range(n_level):
             send_sum(1, i).start()
+
+    @pl.when(skips)
+    def _():
+        for i, there in enumerate(groups[1]):
+
+            @pl.when(jnp.logical_not((there[0] == first[0]) & (there[1] == first[1])))
+            def _(i=i):
+                send_sum(1, i).start()
 
     @pl.when(is_first)
     def _():

time: 25.5 us -> 25.4 us (level)
  the two profiles are of different devices: /device:TPU:1 before, /device:TPU:8 now
where the time goes in v5:
time: 25.4 us; the launch traced here: 25.3 us
  Pallas kernels  24.7 us (97%)
  between operations  0.64 us (3%)
    pallas_call x1, Pallas kernels, shards(): pl.pallas_call(derive, out_shape=(pltpu.VMEM(shape, f32), pltpu.VMEM((com...  21.9 us
    pallas_call x1, Pallas kernels, shards(): pl.pallas_call(deliver, out_shape=(jax.ShapeDtypeStruct(shape, f32), jax....  2.72 us

profile of v5, /device:TPU:8, one launch (start us, length us, event | category | flops | bytes accessed | tf_op | source)
XLA Modules:
  0.0 25.3 jit_solution(3887337455198108182)
XLA Ops:
  0.6 21.9 %derive.1 = (f32[24,256,256]{2,1,0:T(8,128)S(1)}, f32[3,8]{1,0:T(4,128)S(1)}) custom-call(f32[24,256,256]{2,1,0:T(8,128)} %bitcast.2, f32[256,256]{1,0:T(8,128)} %constant.4.clone.matrix_hbm, f32[4,96,128]{2,1,0:T(8,128)} %constant.5.clone.column_hbm), custom_call_target="tpu_custom_call" | custom-call | tf_op jit(solution)/shard_map/derive/pallas_call | solution.py:355
  22.6 2.7 %deliver.1 = (f32[24,256,256]{2,1,0:T(8,128)}, f32[3,8]{1,0:T(4,128)}) custom-call(f32[24,256,256]{2,1,0:T(8,128)S(1)} %get-tuple-element.6.d_vmem, f32[3,8]{1,0:T(4,128)S(1)} %get-tuple-element.7.e_vmem), custom_call_target="tpu_custom_call" | custom-call | tf_op jit(solution)/shard_map/deliver/pallas_call | solution.py:389

commit v6 on v5

--- a/solution.py
+++ b/solution.py
@@ -23,7 +23,10 @@
 
 SIZES = {"x": 4, "y": 4, "z": 8, "core": 2}
 PHASES = (("x", "y"), ("z", "core"))
-AHEAD = {"x": 0, "y": 0, "z": 0, "core": 1}
+AHEAD = (
+    (0, 0, 0, 1), (0, 1, 0, 0), (0, 1, 0, 1), (0, 0, 1, 0), (0, 0, 1, 1), (1, 0, 0, 0), (1, 0, 0, 1),
+    (0, 2, 0, 0), (0, 2, 0, 1), (0, 3, 0, 0), (0, 3, 0, 1),
+)
 FAR = range(3, 8)
 MESH = pl.DeviceIdType.MESH
 LANES = 128
@@ -66,13 +69,16 @@
     return [at(**dict(zip(axes, offset))) for offset in offsets]
 
 
-def far_devices():
+def place_of(x, y, z, core):
+    return z * SIZES["y"] + y, x * SIZES["core"] + core
+
+
+def far_devices(x=0, y=0, z=0, core=0):
     found = []
-    for z, y, x, core in itertools.product(FAR, *(range(SIZES[a]) for a in ("y", "x", "core"))):
-        place = {"x": x, "y": y, "z": z, "core": core}
-        away = sum(hops(abs(place[a] - AHEAD[a]), a) for a in place)
-        found.append((-away, z * SIZES["y"] + y, x * SIZES["core"] + core))
-    return [there for _, *there in sorted(found)]
+    for there in itertools.product(*(range(SIZES[a]) for a in ("x", "y")), FAR, range(SIZES["core"])):
+        away = sum(hops(abs(to - at), a) for to, at, a in zip(there, (x, y, z, core), ("x", "y", "z", "core")))
+        found.append((-away, *place_of(*there)))
+    return [tuple(there) for _, *there in sorted(found)]
 
 
 def tables(points):
@@ -137,15 +143,17 @@
     for there in known:
         signal(barrier, there)
 
-    first = (AHEAD["z"] * SIZES["y"] + AHEAD["y"], AHEAD["x"] * SIZES["core"] + AHEAD["core"])
-    is_first = (gx == first[0]) & (gz == first[1])
+    ahead = [place_of(*there) for there in AHEAD]
+    is_ahead = functools.reduce(jnp.logical_or, ((gx == there[0]) & (gz == there[1]) for there in ahead))
     low, high_end = FAR.start * SIZES["y"], FAR.stop * SIZES["y"]
     is_far = (gx >= low) & (gx < high_end)
 
-    @pl.when(is_first)
-    def _():
-        for there in far_devices():
-            signal(barrier, there)
+    for place, there in zip(AHEAD, ahead):
+
+        @pl.when((gx == there[0]) & (gz == there[1]))
+        def _(place=place):
+            for target in far_devices(*place):
+                signal(barrier, target)
 
     constants[0].wait()
 
@@ -179,7 +187,7 @@
 
         lax.fori_loop(0, per_part // PIECE, summarise_piece, 0)
         if part == parts - 2:
-            pl.semaphore_wait(barrier, len(known) + is_far.astype(jnp.int32))
+            pl.semaphore_wait(barrier, len(known) + len(AHEAD) * is_far.astype(jnp.int32))
         if part >= parts - 2:
             for ready in range(parts - 1) if part == parts - 2 else (part,):
                 for i in range(2):
@@ -240,10 +248,10 @@
 
     n_far = direct.shape[0]
 
-    def send_direct():
+    def send_direct(target):
         return pltpu.make_async_remote_copy(
             src_ref=shares.at[0, pl.ds(len(groups[0]), 1)], dst_ref=direct.at[pl.ds((gx - low) * ROW + gz, 1)],
-            send_sem=direct_send, recv_sem=direct_recv, device_id=first, device_id_type=MESH,
+            send_sem=direct_send, recv_sem=direct_recv, device_id=target, device_id_type=MESH,
         )
 
     def send_sum(phase, i):
@@ -259,18 +267,28 @@
         return pltpu.make_async_copy(part, part, semaphore.at[phase])
 
     n_near, n_level = len(groups[0]), len(groups[1])
-    skips = is_far & (lax.rem(gx, SIZES["y"]) == AHEAD["y"]) & (lax.div(gz, SIZES["core"]) == AHEAD["x"])
+    skips = {}
+    for x, y, _, _ in AHEAD:
+        skips.setdefault((x, y), sum(place[:2] == (x, y) for place in AHEAD))
+    here = lax.rem(gx, SIZES["y"]), lax.div(gz, SIZES["core"])
+    skip = {xy: is_far & (here[0] == xy[1]) & (here[1] == xy[0]) for xy in skips}
+    skips_none = jnp.logical_not(functools.reduce(jnp.logical_or, skip.values()))
     n_skip = len(FAR) * SIZES["core"]
 
     shares[0, n_near : n_near + 1, :] = share
 
     @pl.when(is_far)
     def _():
-        send_direct().start()
+        send_direct(ahead[0]).start()
 
     pl.semaphore_wait(near_sem, len(row) + 2)
     for i in range(n_near):
         send_sum(0, i).start()
+
+    @pl.when(is_far)
+    def _():
+        for target in ahead[1:]:
+            send_direct(target).start()
 
     signal(mate_sem, mate)
 
@@ -290,26 +308,30 @@
     rows_of(0, n_near, sum_recv).wait()
     shares[1, n_level : n_level + 1, :] = jnp.sum(shares[0], axis=0, keepdims=True)
     pl.semaphore_wait(mate_sem, 1)
-    @pl.when(jnp.logical_not(skips))
+    @pl.when(skips_none)
     def _():
         for i in range(n_level):
             send_sum(1, i).start()
 
-    @pl.when(skips)
-    def _():
-        for i, there in enumerate(groups[1]):
-
-            @pl.when(jnp.logical_not((there[0] == first[0]) & (there[1] == first[1])))
-            def _(i=i):
-                send_sum(1, i).start()
-
-    @pl.when(is_first)
+    for xy, condition in skip.items():
+
+        @pl.when(condition)
+        def _(xy=xy):
+            kept = [there for place, there in zip(AHEAD, ahead) if place[:2] == xy]
+            for i, there in enumerate(groups[1]):
+                spared = functools.reduce(jnp.logical_or, ((there[0] == k[0]) & (there[1] == k[1]) for k in kept))
+
+                @pl.when(jnp.logical_not(spared))
+                def _(i=i):
+                    send_sum(1, i).start()
+
+    @pl.when(is_ahead)
     def _():
         rows_of(1, n_level - n_skip, sum_recv).wait()
         pltpu.make_async_copy(direct, direct, direct_recv).wait()
         extra[...] = jnp.sum(direct[...], axis=0, keepdims=True)
 
-    @pl.when(jnp.logical_not(is_first))
+    @pl.when(jnp.logical_not(is_ahead))
     def _():
         rows_of(1, n_level, sum_recv).wait()
 
@@ -321,17 +343,20 @@
         e_ref[i : i + 1, :] = total[:, i * per_row : (i + 1) * per_row]
     rows_of(0, n_near, sum_send).wait()
 
-    @pl.when(skips)
-    def _():
-        rows_of(1, n_level - 1, sum_send).wait()
-
-    @pl.when(jnp.logical_not(skips))
+    @pl.when(skips_none)
     def _():
         rows_of(1, n_level, sum_send).wait()
 
+    for xy, condition in skip.items():
+
+        @pl.when(condition)
+        def _(xy=xy):
+            rows_of(1, n_level - skips[xy], sum_send).wait()
+
     @pl.when(is_far)
     def _():
-        send_direct().wait_send()
+        part = direct.at[pl.ds(0, len(ahead))]
+        pltpu.make_async_copy(part, part, direct_send).wait()
 
 
 def deliver(d_vmem, e_vmem, d_hbm, e_hbm, sem):

time: 25.4 us -> 24.9 us (0.980)
  the two profiles are of different devices: /device:TPU:8 before, /device:TPU:1 now
where the time goes in v6:
time: 24.9 us; the launch traced here: 24.8 us
  Pallas kernels  24.2 us (97%)
  between operations  0.64 us (3%)
    pallas_call x1, Pallas kernels, shards(): pl.pallas_call(derive, out_shape=(pltpu.VMEM(shape, f32), pltpu.VMEM((com...  21.5 us
    pallas_call x1, Pallas kernels, shards(): pl.pallas_call(deliver, out_shape=(jax.ShapeDtypeStruct(shape, f32), jax....  2.72 us

profile of v6, /device:TPU:1, one launch (start us, length us, event | category | flops | bytes accessed | tf_op | source)
XLA Modules:
  0.0 24.8 jit_solution(3028629082352147271)
XLA Ops:
  0.6 21.5 %derive.1 = (f32[24,256,256]{2,1,0:T(8,128)S(1)}, f32[3,8]{1,0:T(4,128)S(1)}) custom-call(f32[24,256,256]{2,1,0:T(8,128)} %bitcast.2, f32[256,256]{1,0:T(8,128)} %constant.4.clone.matrix_hbm, f32[4,96,128]{2,1,0:T(8,128)} %constant.5.clone.column_hbm), custom_call_target="tpu_custom_call" | custom-call | tf_op jit(solution)/shard_map/derive/pallas_call | solution.py:380
  22.1 2.7 %deliver.1 = (f32[24,256,256]{2,1,0:T(8,128)}, f32[3,8]{1,0:T(4,128)}) custom-call(f32[24,256,256]{2,1,0:T(8,128)S(1)} %get-tuple-element.6.d_vmem, f32[3,8]{1,0:T(4,128)S(1)} %get-tuple-element.7.e_vmem), custom_call_target="tpu_custom_call" | custom-call | tf_op jit(solution)/shard_map/deliver/pallas_call | solution.py:414

commit v7 on v6

--- a/solution.py
+++ b/solution.py
@@ -25,7 +25,8 @@
 PHASES = (("x", "y"), ("z", "core"))
 AHEAD = (
     (0, 0, 0, 1), (0, 1, 0, 0), (0, 1, 0, 1), (0, 0, 1, 0), (0, 0, 1, 1), (1, 0, 0, 0), (1, 0, 0, 1),
-    (0, 2, 0, 0), (0, 2, 0, 1), (0, 3, 0, 0), (0, 3, 0, 1),
+    (0, 2, 0, 0), (0, 2, 0, 1), (0, 3, 0, 0), (0, 3, 0, 1), (0, 0, 2, 0), (0, 0, 2, 1),
+    (0, 1, 1, 0), (0, 1, 1, 1), (1, 0, 1, 0), (1, 0, 1, 1),
 )
 FAR = range(3, 8)
 MESH = pl.DeviceIdType.MESH
@@ -73,12 +74,12 @@
     return z * SIZES["y"] + y, x * SIZES["core"] + core
 
 
-def far_devices(x=0, y=0, z=0, core=0):
+def far_devices(x=0, y=0):
     found = []
     for there in itertools.product(*(range(SIZES[a]) for a in ("x", "y")), FAR, range(SIZES["core"])):
-        away = sum(hops(abs(to - at), a) for to, at, a in zip(there, (x, y, z, core), ("x", "y", "z", "core")))
-        found.append((-away, *place_of(*there)))
-    return [tuple(there) for _, *there in sorted(found)]
+        away = sum(hops(abs(to - at), a) for to, at, a in zip(there, (x, y), ("x", "y")))
+        found.append((there[2], away, *place_of(*there)))
+    return [tuple(there) for _, _, *there in sorted(found)]
 
 
 def tables(points):
@@ -152,7 +153,7 @@
 
         @pl.when((gx == there[0]) & (gz == there[1]))
         def _(place=place):
-            for target in far_devices(*place):
+            for target in far_devices(*place[:2]):
                 signal(barrier, target)
 
     constants[0].wait()

time: 24.9 us -> 24.9 us (level)
  no operation moved by 1% of the time
where the time goes in v7:
time: 24.9 us; the launch traced here: 24.8 us
  Pallas kernels  24.2 us (97%)
  between operations  0.64 us (3%)
    pallas_call x1, Pallas kernels, shards(): pl.pallas_call(derive, out_shape=(pltpu.VMEM(shape, f32), pltpu.VMEM((com...  21.5 us
    pallas_call x1, Pallas kernels, shards(): pl.pallas_call(deliver, out_shape=(jax.ShapeDtypeStruct(shape, f32), jax....  2.72 us

profile of v7, /device:TPU:1, one launch (start us, length us, event | category | flops | bytes accessed | tf_op | source)
XLA Modules:
  0.0 24.8 jit_solution(14041943939999915389)
XLA Ops:
  0.6 21.5 %derive.1 = (f32[24,256,256]{2,1,0:T(8,128)S(1)}, f32[3,8]{1,0:T(4,128)S(1)}) custom-call(f32[24,256,256]{2,1,0:T(8,128)} %bitcast.2, f32[256,256]{1,0:T(8,128)} %constant.4.clone.matrix_hbm, f32[4,96,128]{2,1,0:T(8,128)} %constant.5.clone.column_hbm), custom_call_target="tpu_custom_call" | custom-call | tf_op jit(solution)/shard_map/derive/pallas_call | solution.py:381
  22.1 2.7 %deliver.1 = (f32[24,256,256]{2,1,0:T(8,128)}, f32[3,8]{1,0:T(4,128)}) custom-call(f32[24,256,256]{2,1,0:T(8,128)S(1)} %get-tuple-element.6.d_vmem, f32[3,8]{1,0:T(4,128)S(1)} %get-tuple-element.7.e_vmem), custom_call_target="tpu_custom_call" | custom-call | tf_op jit(solution)/shard_map/deliver/pallas_call | solution.py:415

commit v8 on v7

--- a/solution.py
+++ b/solution.py
@@ -105,7 +105,7 @@
 def derive(
     v_hbm, matrix_hbm, column_hbm, d_ref, e_ref,
     v, matrix, split, columns, out, got, rows, tots, shares, load_sem, const_sem, halo_send, halo_recv, sum_send, sum_recv,
-    direct, extra, direct_send, direct_recv, near_sem, mate_sem,
+    direct, total, direct_send, direct_recv, near_sem, mate_sem,
 ):
     planes, points, _ = v.shape
     parts, per_part = out.shape[1], out.shape[3]
@@ -117,7 +117,6 @@
     groups = [partners(at, axes) for axes in PHASES]
 
     shares[1] = jnp.zeros_like(shares[1])
-    extra[...] = jnp.zeros_like(extra)
 
     constants = [
         pltpu.make_async_copy(source, target, const_sem.at[i])
@@ -235,11 +234,11 @@
         for side, sign in ((0, 1.0), (1, -1.0)):
             own, inner, edge = out[side, part, 0], rows[side, span, :], got[side, part, 0]
             jump = sign * (inner - edge)
-            total = jump + got[side, part, 1] + (sign * ROOT) * (own - edge)
-            energy = energy + 2.0 * (TAIL * total * rows[4 + side, span, :] + BUMP * jump * rows[2 + side, span, :])
-            energy = energy + (TAIL * TAIL * squares) * total * total
-            energy = energy + (2.0 * TAIL * BUMP) * total * jump + (BUMP * BUMP) * jump * jump
-            tots[side, span, :] = TAIL * total
+            reach_sum = jump + got[side, part, 1] + (sign * ROOT) * (own - edge)
+            energy = energy + 2.0 * (TAIL * reach_sum * rows[4 + side, span, :] + BUMP * jump * rows[2 + side, span, :])
+            energy = energy + (TAIL * TAIL * squares) * reach_sum * reach_sum
+            energy = energy + (2.0 * TAIL * BUMP) * reach_sum * jump + (BUMP * BUMP) * jump * jump
+            tots[side, span, :] = TAIL * reach_sum
             tots[2 + side, span, :] = BUMP * jump
         sums.append(jnp.sum(energy[:, :LANES] + energy[:, LANES:], axis=1, keepdims=True))
 
@@ -330,18 +329,18 @@
     def _():
         rows_of(1, n_level - n_skip, sum_recv).wait()
         pltpu.make_async_copy(direct, direct, direct_recv).wait()
-        extra[...] = jnp.sum(direct[...], axis=0, keepdims=True)
+        total[...] = jnp.sum(jnp.concatenate([shares[1], direct[...]], axis=0), axis=0, keepdims=True)
 
     @pl.when(jnp.logical_not(is_ahead))
     def _():
         rows_of(1, n_level, sum_recv).wait()
-
-    total = jnp.sum(shares[1], axis=0, keepdims=True) + extra[...]
+        total[...] = jnp.sum(shares[1], axis=0, keepdims=True)
+
     count = float(points * ring * 2 * LANES * lax.axis_size("gz"))
-    total = total * (1.0 / count)
+    mean = total[...] * (1.0 / count)
     per_row = e_ref.shape[1]
     for i in range(e_ref.shape[0]):
-        e_ref[i : i + 1, :] = total[:, i * per_row : (i + 1) * per_row]
+        e_ref[i : i + 1, :] = mean[:, i * per_row : (i + 1) * per_row]
     rows_of(0, n_near, sum_send).wait()
 
     @pl.when(skips_none)

time: 24.9 us -> 24.9 us (level)
  no operation moved by 1% of the time
where the time goes in v8:
time: 24.9 us; the launch traced here: 24.8 us
  Pallas kernels  24.2 us (97%)
  between operations  0.64 us (3%)
    pallas_call x1, Pallas kernels, shards(): pl.pallas_call(derive, out_shape=(pltpu.VMEM(shape, f32), pltpu.VMEM((com...  21.5 us
    pallas_call x1, Pallas kernels, shards(): pl.pallas_call(deliver, out_shape=(jax.ShapeDtypeStruct(shape, f32), jax....  2.72 us

profile of v8, /device:TPU:1, one launch (start us, length us, event | category | flops | bytes accessed | tf_op | source)
XLA Modules:
  0.0 24.8 jit_solution(17871665671308537871)
XLA Ops:
  0.6 21.5 %derive.1 = (f32[24,256,256]{2,1,0:T(8,128)S(1)}, f32[3,8]{1,0:T(4,128)S(1)}) custom-call(f32[24,256,256]{2,1,0:T(8,128)} %bitcast.2, f32[256,256]{1,0:T(8,128)} %constant.4.clone.matrix_hbm, f32[4,96,128]{2,1,0:T(8,128)} %constant.5.clone.column_hbm), custom_call_target="tpu_custom_call" | custom-call | tf_op jit(solution)/shard_map/derive/pallas_call | solution.py:380
  22.1 2.7 %deliver.1 = (f32[24,256,256]{2,1,0:T(8,128)}, f32[3,8]{1,0:T(4,128)}) custom-call(f32[24,256,256]{2,1,0:T(8,128)S(1)} %get-tuple-element.6.d_vmem, f32[3,8]{1,0:T(4,128)S(1)} %get-tuple-element.7.e_vmem), custom_call_target="tpu_custom_call" | custom-call | tf_op jit(solution)/shard_map/deliver/pallas_call | solution.py:414
